TPU v7x, 32 devices: a whole 2x2x4 slice. The times are simulated.
32 devices in a mesh: lon: 8 (over z, y), head: 4 (over x, core).
Axes of the slice: x: 2, y: 2, z: 4, core: 2. Of those that a mesh axis runs over, the one named last changes fastest.
Arguments:
- tokens: bfloat16 [48, 128, 1024], P(None, ('lon', 'head')), may hold values from -6 to 6
- norm_gain: float32 [1024], replicated, may hold values from 0.25 to 1.75
- w_qkv: bfloat16 [1024, 3072], replicated, may hold values from -4 to 4
- w_out: bfloat16 [1024, 1024], replicated, may hold values from -0.1875 to 0.1875
- widths: int32 [6, 8], replicated, may hold values from 0 to 2, as said below
Outputs:
- mixed: bfloat16 [48, 128, 1024], P(None, ('lon', 'head'))
Inputs may be any that keep to these rules, and one draw needn't show every extreme that they name: widths[b, c] is the longitude half-width in blocks of the neighbourhood of query block (b, c).
All inputs are finite; a program needn't handle non-finite values.
Results may differ from a plain program's by a relative error of at most 0.0092.
Values may be sent and summed in bfloat16 or wider, within the bound.
A program may use at most 64 MiB of HBM per device.

v0:
```python
import jax
import jax.numpy as jnp
from jax import lax
from jax.sharding import PartitionSpec as P

H = 8
HD = 128
LATITUDE_BANDS = 6
BLAT = 8
BLON = 16
REACH = 2


def shifted(array, axis, by):
    count = lax.axis_size(axis)
    return lax.ppermute(array, axis, [(i, (i + by) % count) for i in range(count)])


def per_device(tokens, norm_gain, w_qkv, w_out, widths):
    lat_rows, lon_tok, width = tokens.shape
    n_head = lax.axis_size("head")
    pairs = LATITUDE_BANDS * H // n_head
    sector = lon_tok * n_head
    sblocks = sector // BLON
    block_len = BLAT * BLON
    scale = HD ** (-0.5)
    x32 = tokens.astype(jnp.float32)
    scale_rms = lax.rsqrt(jnp.mean(x32 * x32, axis=-1, keepdims=True) + 1e-05)
    normed = (x32 * scale_rms * norm_gain).astype(jnp.bfloat16)
    qkv = jnp.dot(normed.reshape(-1, width), w_qkv, preferred_element_type=jnp.float32).astype(
        jnp.bfloat16
    )
    qkv = (
        qkv.reshape(LATITUDE_BANDS, BLAT, lon_tok, 3, H, HD)
        .transpose(0, 4, 1, 2, 3, 5)
        .reshape(LATITUDE_BANDS * H, BLAT, lon_tok, 3 * HD)
    )
    mine = lax.all_to_all(qkv, "head", split_axis=0, concat_axis=2, tiled=True)
    blocks = (
        mine.reshape(pairs, BLAT, sblocks, BLON, 3 * HD)
        .transpose(0, 2, 1, 3, 4)
        .reshape(pairs, sblocks, block_len, 3 * HD)
    )
    query = blocks[..., :HD]
    keyval = blocks[..., HD:]
    pair_ids = lax.axis_index("head") * pairs + jnp.arange(pairs, dtype=jnp.int32)
    band_ids = pair_ids // H
    onehot = (band_ids[:, None] == jnp.arange(LATITUDE_BANDS, dtype=jnp.int32)[None, :]).astype(
        jnp.int32
    )
    band_widths = jnp.sum(onehot[:, :, None] * widths[None, :, :], axis=1)
    reach = lax.dynamic_slice_in_dim(band_widths, lax.axis_index("lon") * sblocks, sblocks, 1)
    q_index = jnp.arange(sblocks, dtype=jnp.int32)

    def attend(state, pieces, shift_blocks):
        top, total, accum = state
        keys = pieces[..., :HD]
        value_entries = pieces[..., HD:]
        scores = (
            jnp.einsum("pqtd,pkud->pqtku", query, keys, preferred_element_type=jnp.float32) * scale
        )
        offset = shift_blocks + q_index[None, :] - q_index[:, None]
        allowed = jnp.abs(offset)[None, :, :] <= reach[:, :, None]
        allowed = allowed[:, :, None, :, None]
        new_top = jnp.maximum(top, jnp.max(jnp.where(allowed, scores, -1e30), axis=(3, 4)))
        expo = jnp.where(allowed, jnp.exp(scores - new_top[..., None, None]), 0.0)
        factor = jnp.exp(top - new_top)
        total = total * factor + jnp.sum(expo, axis=(3, 4))
        update = jnp.einsum(
            "pqtku,pkud->pqtd",
            expo.astype(jnp.bfloat16),
            value_entries,
            preferred_element_type=jnp.float32,
        )
        accum = accum * factor[..., None] + update
        return (new_top, total, accum)

    start = (
        jnp.full((pairs, sblocks, block_len), -1e30, jnp.float32),
        jnp.zeros((pairs, sblocks, block_len), jnp.float32),
        jnp.zeros((pairs, sblocks, block_len, HD), jnp.float32),
    )
    state = attend(start, keyval, 0)
    travel = shifted(keyval, "lon", -REACH)
    state = attend(state, travel, REACH * sblocks)
    for step in range(1, 2 * REACH + 1):
        travel = shifted(travel, "lon", 1)
        distance = REACH - step
        if distance != 0:
            state = attend(state, travel, distance * sblocks)
    top, total, accum = state
    result = (accum / total[..., None]).astype(jnp.bfloat16)
    result = (
        result.reshape(pairs, sblocks, BLAT, BLON, HD)
        .transpose(0, 2, 1, 3, 4)
        .reshape(pairs, BLAT, sector, HD)
    )
    back = lax.all_to_all(result, "head", split_axis=2, concat_axis=0, tiled=True)
    back = (
        back.reshape(LATITUDE_BANDS, H, BLAT, lon_tok, HD)
        .transpose(0, 2, 3, 1, 4)
        .reshape(lat_rows * lon_tok, width)
    )
    proj = jnp.dot(back, w_out, preferred_element_type=jnp.float32)
    return (x32.reshape(-1, width) + proj).astype(jnp.bfloat16).reshape(lat_rows, lon_tok, width)


def solution(mesh):
    placed = (P(None, ("lon", "head"), None), P(), P(), P(), P())
    return jax.shard_map(
        per_device,
        mesh=mesh,
        in_specs=placed,
        out_specs=P(None, ("lon", "head"), None),
        check_vma=False,
    )
```

profile of v0, /device:TPU:0, one launch (start us, length us, event | category | flops | bytes accessed | tf_op | source)
XLA Modules:
  0.0 158.6 jit_solution(18192406514715826418)
XLA Ops:
  0.0 1.4 multiply_reduce_fusion
  1.4 1.3 multiply_convert_fusion
  2.8 4.2 %fusion = bf16[24,8,24,128]{3,1,2,0:T(8,128)(2,1)S(1)} fusion(bf16[192,1024]{1,0:T(8,128)(2,1)S(1)} %reshape.429, bf16[1024,3072]{1,0:T(8,128)(2,1)} %param.7), kind=kOutput, calls=%fused_computation.2 | convolution fusion | flops 1208549376 | bytes 7864320 | tf_op jit(solution)/shard_map/dot_general | solution.py:30
  7.2 2.0 %copy.90 = bf16[6,8,4,3,8,128]{5,3,1,2,4,0:T(4,128)(2,1)} copy(bf16[6,8,4,3,8,128]{5,4,3,2,1,0:T(8,128)(2,1)S(1)} %bitcast.92) | data formatting | bytes 2359296 | tf_op jit(solution)/shard_map/reshape | solution.py:34
  9.2 3.4 %reshape.431 = bf16[48,8,4,384]{3,1,2,0:T(8,128)(2,1)S(1)} reshape(bf16[6,8,8,4,3,128]{5,4,2,3,1,0:T(4,128)(2,1)} %bitcast.90) | data formatting | bytes 2359296 | tf_op jit(solution)/shard_map/reshape | solution.py:36
  12.6 19.9 %all_to_all.30 = bf16[48,8,4,384]{3,1,2,0:T(8,128)(2,1)S(1)} all-to-all(bf16[48,8,4,384]{3,1,2,0:T(8,128)(2,1)S(1)} %reshape.431), channel_id=1, replica_groups=mesh['lon'=8,'head'=4] {'head'}, dimensions={0} | all-to-all | bytes 2359296 | tf_op jit(solution)/shard_map/all_to_all | solution.py:38
  32.5 1.5 copy.66
  34.0 2.4 %reshape_transpose_reshape.6 = bf16[12,1,128,384]{3,2,0,1:T(8,128)(2,1)S(1)} reshape(bf16[12,8,4,4,384]{4,3,2,1,0:T(4,128)(2,1)} %copy.66) | data formatting | bytes 2359296 | tf_op jit(solution)/shard_map/reshape;transpose;reshape | solution.py:42
  36.4 3.7 %collective-permute-start = (bf16[12,1,128,256]{3,2,0,1:T(8,128)(2,1)S(1)}, bf16[12,1,128,256]{3,2,0,1:T(8,128)(2,1)S(1)}, u32[]{:S(2)}, u32[]{:S(2)}) collective-permute-start(bf16[12,1,128,256]{3,2,0,1:T(8,128)(2,1)S(1)} %slice.53), channel_id=1, source_target_pairs={{0,24},{4,28},{8,0},{12,4},{16,8},{20,12},{24,16},{28,20},{1,25},{... | collective-permute-start | bytes 2359304 | tf_op jit(solution)/shard_map/ppermute | solution.py:16
  40.1 16.4 %collective-permute-done = bf16[12,1,128,256]{3,2,0,1:T(8,128)(2,1)S(1)} collective-permute-done((bf16[12,1,128,256]{3,2,0,1:T(8,128)(2,1)S(1)}, bf16[12,1,128,256]{3,2,0,1:T(8,128)(2,1)S(1)}, u32[]{:S(2)}, u32[]{:S(2)}) %collective-permute-start) | collective-permute-done | bytes 786464 | tf_op jit(solution)/shard_map/ppermute | solution.py:16
  56.5 0.9 copy-done.2
  57.4 1.5 collective-permute-start.1
  58.9 20.1 %collective-permute-done.1 = bf16[12,1,128,256]{3,2,0,1:T(8,128)(2,1)} collective-permute-done((bf16[12,1,128,256]{3,2,0,1:T(8,128)(2,1)S(1)}, bf16[12,1,128,256]{3,2,0,1:T(8,128)(2,1)}, u32[]{:S(2)}, u32[]{:S(2)}) %collective-permute-start.1) | collective-permute-done | bytes 786464 | tf_op jit(solution)/shard_map/ppermute | solution.py:16
  79.0 20.3 %collective-permute-done.2 = bf16[12,1,128,256]{3,2,0,1:T(8,128)(2,1)} collective-permute-done((bf16[12,1,128,256]{3,2,0,1:T(8,128)(2,1)}, bf16[12,1,128,256]{3,2,0,1:T(8,128)(2,1)}, u32[]{:S(2)}, u32[]{:S(2)}) %collective-permute-start.2) | collective-permute-done | bytes 786464 | tf_op jit(solution)/shard_map/ppermute | solution.py:16
  99.9 0.6 copy-done.3
  100.5 0.4 select_reduce_fusion.3
  100.9 17.9 %collective-permute-done.3 = bf16[12,1,128,256]{3,2,0,1:T(8,128)(2,1)} collective-permute-done((bf16[12,1,128,256]{3,2,0,1:T(8,128)(2,1)}, bf16[12,1,128,256]{3,2,0,1:T(8,128)(2,1)}, u32[]{:S(2)}, u32[]{:S(2)}) %collective-permute-start.3) | collective-permute-done | bytes 786464 | tf_op jit(solution)/shard_map/ppermute | solution.py:16
  118.8 1.4 select_reduce_fusion.2
  120.4 1.4 fusion.12
  121.8 15.4 %collective-permute-done.4 = bf16[12,1,128,256]{3,2,0,1:T(8,128)(2,1)S(1)} collective-permute-done((bf16[12,1,128,256]{3,2,0,1:T(8,128)(2,1)}, bf16[12,1,128,256]{3,2,0,1:T(8,128)(2,1)S(1)}, u32[]{:S(2)}, u32[]{:S(2)}) %collective-permute-start.4) | collective-permute-done | bytes 786464 | tf_op jit(solution)/shard_map/ppermute | solution.py:16
  137.2 0.4 fusion.10
  138.0 1.1 fusion.1
  139.2 0.5 fusion.2
  139.7 1.5 fusion.3
  141.2 1.5 fusion.4
  142.8 0.5 fusion.7
  143.3 0.8 copy.72
  144.2 4.2 %all-to-all-start.1 = ((bf16[12,8,16,128]{3,1,0,2:T(8,128)(2,1)}), bf16[12,8,16,128]{3,1,0,2:T(8,128)(2,1)}, u32[]{:S(2)}, u32[]{:S(2)}) async-start(bf16[12,8,16,128]{3,1,0,2:T(8,128)(2,1)} %copy.72), calls=%async_computation.1 | async-start | bytes 786432 | tf_op jit(solution)/shard_map/all_to_all | solution.py:98
  148.4 7.5 %all-to-all-done.1 = bf16[12,8,16,128]{3,1,0,2:T(8,128)(2,1)} async-done(((bf16[12,8,16,128]{3,1,0,2:T(8,128)(2,1)}), bf16[12,8,16,128]{3,1,0,2:T(8,128)(2,1)}, u32[]{:S(2)}, u32[]{:S(2)}) %all-to-all-start.1) | async-done | bytes 393248 | tf_op jit(solution)/shard_map/all_to_all | solution.py:98
  155.9 1.1 copy.74
  157.2 0.6 fusion.6
  157.8 0.9 reshape.445
  (27 shorter events, 1.6 us)
Async XLA Ops:
  0.0 157.2 %copy-start = (bf16[1024,1024]{1,0:T(8,128)(2,1)S(1)}, bf16[1024,1024]{1,0:T(8,128)(2,1)}, u32[]{:S(2)}) copy-start(bf16[1024,1024]{1,0:T(8,128)(2,1)} %param.8) | copy-start | bytes 6291460
  36.4 63.0 %copy-start.4 = (s32[6,8]{1,0:T(8,128)S(1)}, s32[6,8]{1,0:T(8,128)}, u32[]{:S(2)}) copy-start(s32[6,8]{1,0:T(8,128)} %param.9) | copy-start | bytes 580
  36.4 20.1 %collective-permute-start = (bf16[12,1,128,256]{3,2,0,1:T(8,128)(2,1)S(1)}, bf16[12,1,128,256]{3,2,0,1:T(8,128)(2,1)S(1)}, u32[]{:S(2)}, u32[]{:S(2)}) collective-permute-start(bf16[12,1,128,256]{3,2,0,1:T(8,128)(2,1)S(1)} %slice.53), channel_id=1, source_target_pairs={{0,24},{4,28},{8,0},{12,4},{16,8},{20,12},{24,16},{28,20},{1,25},{... | collective-permute-start | bytes 2359304 | tf_op jit(solution)/shard_map/ppermute | solution.py:16
  56.5 0.9 copy-start.2
  57.4 21.6 %collective-permute-start.1 = (bf16[12,1,128,256]{3,2,0,1:T(8,128)(2,1)S(1)}, bf16[12,1,128,256]{3,2,0,1:T(8,128)(2,1)}, u32[]{:S(2)}, u32[]{:S(2)}) collective-permute-start(bf16[12,1,128,256]{3,2,0,1:T(8,128)(2,1)S(1)} %collective-permute-done), channel_id=1, source_target_pairs={{0,4},{4,8},{8,12},{12,16},{16,20},{20,24},{24,28},{28,0},{1,5},{5... | collective-permute-start | bytes 2359304 | tf_op jit(solution)/shard_map/ppermute | solution.py:16
  79.0 20.4 %collective-permute-start.2 = (bf16[12,1,128,256]{3,2,0,1:T(8,128)(2,1)}, bf16[12,1,128,256]{3,2,0,1:T(8,128)(2,1)}, u32[]{:S(2)}, u32[]{:S(2)}) collective-permute-start(bf16[12,1,128,256]{3,2,0,1:T(8,128)(2,1)} %collective-permute-done.1), channel_id=1, source_target_pairs={{0,4},{4,8},{8,12},{12,16},{16,20},{20,24},{24,28},{28,0},{1,5},{5... | collective-permute-start | bytes 2359304 | tf_op jit(solution)/shard_map/ppermute | solution.py:16
  99.4 19.4 %collective-permute-start.3 = (bf16[12,1,128,256]{3,2,0,1:T(8,128)(2,1)}, bf16[12,1,128,256]{3,2,0,1:T(8,128)(2,1)}, u32[]{:S(2)}, u32[]{:S(2)}) collective-permute-start(bf16[12,1,128,256]{3,2,0,1:T(8,128)(2,1)} %collective-permute-done.2), channel_id=1, source_target_pairs={{0,4},{4,8},{8,12},{12,16},{16,20},{20,24},{24,28},{28,0},{1,5},{5... | collective-permute-start | bytes 2359304 | tf_op jit(solution)/shard_map/ppermute | solution.py:16
  99.4 1.1 copy-start.3
  118.8 18.4 %collective-permute-start.4 = (bf16[12,1,128,256]{3,2,0,1:T(8,128)(2,1)}, bf16[12,1,128,256]{3,2,0,1:T(8,128)(2,1)S(1)}, u32[]{:S(2)}, u32[]{:S(2)}) collective-permute-start(bf16[12,1,128,256]{3,2,0,1:T(8,128)(2,1)} %collective-permute-done.3), channel_id=1, source_target_pairs={{0,4},{4,8},{8,12},{12,16},{16,20},{20,24},{24,28},{28,0},{1,5},{5... | collective-permute-start | bytes 2359304 | tf_op jit(solution)/shard_map/ppermute | solution.py:16
  143.3 5.0 %copy-start.1 = (bf16[48,4,1024]{2,1,0:T(4,128)(2,1)S(1)}, bf16[48,4,1024]{2,1,0:T(4,128)(2,1)}, u32[]{:S(2)}) copy-start(bf16[48,4,1024]{2,1,0:T(4,128)(2,1)} %param.5) | copy-start | bytes 1179652
  144.2 11.7 %all-to-all-start.1 = ((bf16[12,8,16,128]{3,1,0,2:T(8,128)(2,1)}), bf16[12,8,16,128]{3,1,0,2:T(8,128)(2,1)}, u32[]{:S(2)}, u32[]{:S(2)}) async-start(bf16[12,8,16,128]{3,1,0,2:T(8,128)(2,1)} %copy.72), calls=%async_computation.1 | async-start | bytes 786432 | tf_op jit(solution)/shard_map/all_to_all | solution.py:98
where the time goes:
time: 159 us
  waiting for transfers between devices  97.6 us (61%)
  blocking collectives  19.9 us (13%)
  local copies, waits for them, and re-layouts  14.1 us (9%)
  matrix products  14.1 us (9%)
  starting transfers between devices  9.36 us (6%)
  other arithmetic  3.36 us (2%)
    ppermute x5, waiting for transfers between devices, shifted(): lax.ppermute(array, axis, [(i, (i + by) % count) for i in range(count)])  90.1 us
    all_to_all x1, blocking collectives, per_device(): mine = lax.all_to_all(qkv, 'head', split_axis=0, concat_axis=2, tiled=True)  19.9 us
    all_to_all x1, waiting for transfers between devices, per_device(): lax.all_to_all(result, 'head', split_axis=2, concat_axis=0, tiled=True)  7.49 us
    dot_general x5, matrix products, attend(): jnp.einsum('pqtku,pkud->pqtd', expo.astype(jnp.bfloat16), value_entries,...  5.28 us
    ppermute x5, starting transfers between devices, shifted(): lax.ppermute(array, axis, [(i, (i + by) % count) for i in range(count)])  5.18 us
    dot_general x1, matrix products, per_device(): jnp.dot(normed.reshape(-1, width), w_qkv, preferred_element_type=jnp.floa...  4.19 us
    all_to_all x1, starting transfers between devices, per_device(): lax.all_to_all(result, 'head', split_axis=2, concat_axis=0, tiled=True)  4.17 us
    dot_general x5, matrix products, attend(): jnp.einsum('pqtd,pkud->pqtku', query, keys, preferred_element_type=jnp.fl...  4.03 us
  transfers between devices with their start and end apart: 6, of which 6 were waited for; matrix products, arithmetic and copies ran while one was open for 2% of the time, Pallas kernels for 0%

commit v1 on v0

--- a/solution.py
+++ b/solution.py
@@ -1,6 +1,8 @@
 import jax
 import jax.numpy as jnp
 from jax import lax
+from jax.experimental import pallas as pl
+from jax.experimental.pallas import tpu as pltpu
 from jax.sharding import PartitionSpec as P
 
 H = 8
@@ -9,6 +11,12 @@
 BLAT = 8
 BLON = 16
 REACH = 2
+D = H * HD
+BLOCK = BLAT * BLON
+GROUP = LATITUDE_BANDS // 2
+CHUNK = BLOCK // 4
+SLOTS = 2 * REACH + 1
+MESH = pl.DeviceIdType.MESH
 
 
 def shifted(array, axis, by):
@@ -105,10 +113,215 @@
     return (x32.reshape(-1, width) + proj).astype(jnp.bfloat16).reshape(lat_rows, lon_tok, width)
 
 
+def fused_kernel(
+    tok_ref, gain_ref, wqkv_hbm, wout_hbm, widths_ref, out_ref,
+    buf, stage, wq, wo, qs, kv, att, back,
+    wsem, x_send, x_recv, o_send, o_recv, c_send, c_recv, r_send, r_recv,
+):
+    n_lon = lax.axis_size("lon")
+    lon, head = lax.axis_index("lon"), lax.axis_index("head")
+    x, core = head // 2, head % 2
+    y = lon % 2
+    turn = 2 * y - 1
+    far = lax.rem(lon + 2 * turn + n_lon, n_lon)
+    near = lax.rem(lon - 2 * turn + n_lon, n_lon)
+    pair = lon - turn
+    sibling = (lon, 2 * x + 1 - core)
+    across = (lon, 2 * (1 - x) + core)
+    diagonal = (lon, 2 * (1 - x) + 1 - core)
+    partners = [sibling, across, diagonal, (far, head), (near, head), (pair, head)]
+    half_cols = H // 2 * HD
+
+    barrier = pltpu.get_barrier_semaphore()
+    for where in partners:
+        pl.semaphore_signal(barrier, inc=1, device_id=where, device_id_type=MESH)
+
+    loads = []
+    for i in range(3):
+        cols = pl.ds(pl.multiple_of(i * H * HD + core * half_cols, 128), half_cols)
+        loads.append(
+            pltpu.make_async_copy(
+                wqkv_hbm.at[:, cols], wq.at[:, pl.ds(i * half_cols, half_cols)], wsem.at[i]
+            )
+        )
+    loads.append(pltpu.make_async_copy(wout_hbm, wo, wsem.at[3]))
+    for load in loads:
+        load.start()
+
+    def normed(row):
+        part = tok_ref[pl.ds(pl.multiple_of(row, CHUNK), CHUNK), :].astype(jnp.float32)
+        inv = lax.rsqrt(jnp.mean(part * part, axis=-1, keepdims=True) + 1e-05)
+        return (part * inv * gain_ref[...]).astype(jnp.bfloat16)
+
+    def remote(src, dst, send, recv, where):
+        return pltpu.make_async_remote_copy(
+            src_ref=src, dst_ref=dst, send_sem=send, recv_sem=recv,
+            device_id=where, device_id_type=MESH,
+        )
+
+    sent = []
+
+    def begin(copy):
+        copy.start()
+        sent.append(copy)
+        return copy
+
+    x_copies = []
+    for j in range(GROUP):
+        stage[j] = normed(((1 - x) * GROUP + j) * CHUNK)
+        if j == 0:
+            pl.semaphore_wait(barrier, len(partners))
+        x_copies.append(
+            begin(remote(stage.at[j], buf.at[j, 0, core, x], x_send.at[j], x_recv.at[j], across))
+        )
+        buf[j, 0, core, x] = normed((x * GROUP + j) * CHUNK)
+
+    def share(slot, j):
+        half = buf.at[j, slot, core]
+        return begin(remote(half, half, c_send.at[j, slot], c_recv.at[j, slot], sibling))
+
+    def spread(j):
+        x_copies[j].wait_recv()
+        own = buf.at[j, 0, core]
+        copies = {}
+        for slot, where in ((3, (far, head)), (2, (near, head)), (1, (pair, head))):
+            copies[slot] = begin(
+                remote(
+                    own, buf.at[j, slot, core], o_send.at[j, slot], o_recv.at[j, slot], where
+                )
+            )
+        return copies, share(0, j)
+
+    def project(j, first, count):
+        rows = buf[j, first : first + count].reshape(count * 4 * CHUNK, D)
+        made = jnp.dot(rows, wq[:, half_cols:], preferred_element_type=jnp.float32)
+        kv[pl.ds(first * 4 * CHUNK, count * 4 * CHUNK), :] = made.astype(jnp.bfloat16)
+
+    block = lax.broadcasted_iota(jnp.int32, (1, SLOTS * BLOCK), 1) // BLOCK
+    distance = jnp.where(block == 0, 0, jnp.where((block == 1) | (block == 4), 1, 2))
+    scale = HD ** (-0.5)
+
+    pending, own_share = spread(0)
+    returns = []
+    for j in range(GROUP):
+        arrive, shared0 = pending, own_share
+        if j + 1 < GROUP:
+            pending, own_share = None, None
+        shared0.wait_recv()
+        if j == 0:
+            for load in loads[:3]:
+                load.wait()
+        rows = buf[j, 0].reshape(BLOCK, D)
+        qs[...] = jnp.dot(rows, wq[:, :half_cols], preferred_element_type=jnp.float32).astype(
+            jnp.bfloat16
+        )
+        project(j, 0, 1)
+        arrive[3].wait_recv()
+        held = buf.at[j, 3, core]
+        relay = begin(
+            remote(
+                held, buf.at[j, 4, core], o_send.at[j, 4], o_recv.at[j, 4], (pair, head)
+            )
+        )
+        shares = [share(3, j)]
+        if j + 1 < GROUP:
+            pending, own_share = spread(j + 1)
+        arrive[1].wait_recv()
+        shares.append(share(1, j))
+        arrive[2].wait_recv()
+        shares.append(share(2, j))
+        for copy in shares:
+            copy.wait_recv()
+        project(j, 1, 3)
+        relay.wait_recv()
+        share(4, j).wait_recv()
+        project(j, 4, 1)
+
+        allowed = distance <= widths_ref[x * GROUP + j, lon]
+        for h in range(H // 2):
+            cols = pl.ds(h * HD, HD)
+            scores = lax.dot_general(
+                qs[:, cols], kv[:, cols], (((1,), (1,)), ((), ())),
+                preferred_element_type=jnp.float32,
+            )
+            scores = jnp.where(allowed, scores * scale, -1e30)
+            top = jnp.max(scores, axis=1, keepdims=True)
+            expo = jnp.exp(scores - top)
+            total = jnp.sum(expo, axis=1, keepdims=True)
+            mixed = jnp.dot(
+                expo.astype(jnp.bfloat16), kv[:, pl.ds(half_cols + h * HD, HD)],
+                preferred_element_type=jnp.float32,
+            )
+            att[j, :, cols] = (mixed / total).astype(jnp.bfloat16)
+        rows = pl.ds(pl.multiple_of((x * GROUP + j) * CHUNK, CHUNK), CHUNK)
+        for kind, (where, to_x, to_core) in enumerate(
+            ((across, 1 - x, core), (diagonal, 1 - x, 1 - core), (sibling, x, 1 - core))
+        ):
+            piece = pl.ds(pl.multiple_of((to_core * 2 + to_x) * CHUNK, CHUNK), CHUNK)
+            returns.append(
+                begin(
+                    remote(
+                        att.at[j, piece], back.at[core, rows],
+                        r_send.at[j, kind], r_recv.at[j, kind], where,
+                    )
+                )
+            )
+        mine = pl.ds(pl.multiple_of((core * 2 + x) * CHUNK, CHUNK), CHUNK)
+        back[core, rows] = att[j, mine]
+
+    loads[3].wait()
+    for copy in returns:
+        copy.wait_recv()
+    proj = jnp.dot(back[0], wo[:half_cols], preferred_element_type=jnp.float32)
+    proj += jnp.dot(back[1], wo[half_cols:], preferred_element_type=jnp.float32)
+    out_ref[...] = (tok_ref[...].astype(jnp.float32) + proj).astype(jnp.bfloat16)
+    for copy in sent:
+        copy.wait_send()
+
+
+def fused_device(tokens, norm_gain, w_qkv, w_out, widths):
+    lat_rows, lon_tok, width = tokens.shape
+    count = lat_rows * lon_tok
+    half_cols = H // 2 * HD
+    dma = pltpu.SemaphoreType.DMA
+    vmem = pl.BlockSpec(memory_space=pltpu.VMEM)
+    hbm = pl.BlockSpec(memory_space=pl.ANY)
+    out = pl.pallas_call(
+        fused_kernel,
+        out_shape=jax.ShapeDtypeStruct((count, width), jnp.bfloat16),
+        in_specs=[vmem, vmem, hbm, hbm, pl.BlockSpec(memory_space=pltpu.SMEM)],
+        out_specs=vmem,
+        scratch_shapes=[
+            pltpu.VMEM((GROUP, SLOTS, 2, 2, CHUNK, width), jnp.bfloat16),
+            pltpu.VMEM((GROUP, CHUNK, width), jnp.bfloat16),
+            pltpu.VMEM((width, 3 * half_cols), jnp.bfloat16),
+            pltpu.VMEM((width, width), jnp.bfloat16),
+            pltpu.VMEM((BLOCK, half_cols), jnp.bfloat16),
+            pltpu.VMEM((SLOTS * BLOCK, 2 * half_cols), jnp.bfloat16),
+            pltpu.VMEM((GROUP, BLOCK, half_cols), jnp.bfloat16),
+            pltpu.VMEM((2, count, half_cols), jnp.bfloat16),
+            dma((4,)),
+            dma((GROUP,)),
+            dma((GROUP,)),
+            dma((GROUP, SLOTS)),
+            dma((GROUP, SLOTS)),
+            dma((GROUP, SLOTS)),
+            dma((GROUP, SLOTS)),
+            dma((GROUP, 3)),
+            dma((GROUP, 3)),
+        ],
+        compiler_params=pltpu.CompilerParams(
+            collective_id=0, has_side_effects=True, vmem_limit_bytes=48 * 1024 * 1024
+        ),
+    )(tokens.reshape(count, width), norm_gain.reshape(1, width), w_qkv, w_out, widths)
+    return out.reshape(lat_rows, lon_tok, width)
+
+
 def solution(mesh):
     placed = (P(None, ("lon", "head"), None), P(), P(), P(), P())
+    one_block = mesh.shape["lon"] == 8 and mesh.shape["head"] == 4
     return jax.shard_map(
-        per_device,
+        fused_device if one_block else per_device,
         mesh=mesh,
         in_specs=placed,
         out_specs=P(None, ("lon", "head"), None),

time: 159 us -> 48.9 us (0.31)
  waiting for transfers between devices: 97.6 us -> 0 us
  Pallas kernels: 0 us -> 43.7 us
  blocking collectives: 19.9 us -> 0 us
  matrix products: 14.1 us -> 0 us
  starting transfers between devices: 9.36 us -> 0 us
  local copies, waits for them, and re-layouts: 14.1 us -> 4.94 us
  other arithmetic: 3.36 us -> 0 us
    ppermute x5 -> x0, waiting for transfers between devices: 90.1 us -> none  [shifted(): lax.ppermute(array, axis, [(i, (i + by) % count) for i in range(count)])]
    pallas_call x0 -> x1, Pallas kernels: none -> 43.7 us  [fused_device(): pl.pallas_call(fused_kernel, out_shape=jax.ShapeDtypeStruct((count, width...]
    all_to_all x1 -> x0, blocking collectives: 19.9 us -> none  [per_device(): mine = lax.all_to_all(qkv, 'head', split_axis=0, concat_axis=2, tiled=True)]
    dot_general x12 -> x0, matrix products: 14.1 us -> none  [the longest x5 5.28 us: attend(): jnp.einsum('pqtku,pkud->pqtd', expo.astype(jnp.bfloat16), value_entries,...]
    all_to_all x1 -> x0, waiting for transfers between devices: 7.49 us -> none  [per_device(): lax.all_to_all(result, 'head', split_axis=2, concat_axis=0, tiled=True)]
    ppermute x5 -> x0, starting transfers between devices: 5.18 us -> none  [shifted(): lax.ppermute(array, axis, [(i, (i + by) % count) for i in range(count)])]
    reshape x5 -> x2, local copies, waits for them, and re-layouts: 6.38 us -> 1.98 us  [the longest x1 1.08 us: fused_device(): tokens.reshape(count, width)]
    all_to_all x1 -> x0, starting transfers between devices: 4.17 us -> none  [per_device(): lax.all_to_all(result, 'head', split_axis=2, concat_axis=0, tiled=True)]
  transfers between devices with their start and end apart: 6 -> 0, of which waited for: 6 -> 0; matrix products, arithmetic and copies ran while one was open for 2% -> 0% of each run, Pallas kernels for 0% -> 0%
where the time goes in v1:
time: 48.9 us; the launch traced here: 48.7 us
  Pallas kernels  43.7 us (89%)
  local copies, waits for them, and re-layouts  4.94 us (10%)
    pallas_call x1, Pallas kernels, fused_device(): pl.pallas_call(fused_kernel, out_shape=jax.ShapeDtypeStruct((count, width...  43.7 us
    unnamed x6, local copies, waits for them, and re-layouts  2.96 us
    reshape x1, local copies, waits for them, and re-layouts, fused_device(): tokens.reshape(count, width)  1.08 us

profile of v1, /device:TPU:0, one launch (start us, length us, event | category | flops | bytes accessed | tf_op | source)
XLA Modules:
  0.0 48.7 jit_solution(4490560078122169031)
XLA Ops:
  0.0 1.1 %reshape.9.tok_ref = bf16[192,1024]{1,0:T(8,128)(2,1)S(1)} reshape(bf16[48,4,1024]{2,1,0:T(4,128)(2,1)} %param.5) | data formatting | bytes 786432 | tf_op jit(solution)/shard_map/reshape | solution.py:316
  1.1 0.0 copy-start
  1.1 1.6 %copy-done = bf16[1024,1024]{1,0:T(8,128)(2,1)S(1)} copy-done((bf16[1024,1024]{1,0:T(8,128)(2,1)S(1)}, bf16[1024,1024]{1,0:T(8,128)(2,1)}, u32[]{:S(2)}) %copy-start) | copy-done | bytes 2097176
  2.7 0.0 copy-start.1
  2.7 0.7 %copy-done.1 = f32[1024]{0:T(1024)S(1)} copy-done((f32[1024]{0:T(1024)S(1)}, f32[1024]{0:T(1024)}, u32[]{:S(2)}) %copy-start.1) | copy-done | bytes 4120
  3.4 0.0 copy-start.2
  3.4 0.7 %copy-done.2 = s32[6,8]{1,0:T(8,128)S(1)} copy-done((s32[6,8]{1,0:T(8,128)S(1)}, s32[6,8]{1,0:T(8,128)}, u32[]{:S(2)}) %copy-start.2) | copy-done | bytes 216
  4.1 43.7 %shard_map.55 = bf16[192,1024]{1,0:T(8,128)(2,1)S(1)} custom-call(bf16[192,1024]{1,0:T(8,128)(2,1)S(1)} %reshape.9.tok_ref, f32[1,1024]{1,0:T(1,128)S(1)} %bitcast.1, bf16[1024,3072]{1,0:T(8,128)(2,1)} %wqkv_hbm.1, bf16[1024,1024]{1,0:T(8,128)(2,1)S(1)} %copy-done, s32[6,8]{1,0:T(8,128)S(1)} %copy-done.2), custom_call_target="tpu_custom_call" | custom-call | tf_op jit(solution)/shard_map/pallas_call | solution.py:289
  47.8 0.9 %reshape.11 = bf16[48,4,1024]{2,1,0:T(4,128)(2,1)} reshape(bf16[192,1024]{1,0:T(8,128)(2,1)S(1)} %shard_map.55) | data formatting | bytes 786432 | tf_op jit(solution)/shard_map/reshape | solution.py:317
Async XLA Ops:
  1.1 1.6 %copy-start = (bf16[1024,1024]{1,0:T(8,128)(2,1)S(1)}, bf16[1024,1024]{1,0:T(8,128)(2,1)}, u32[]{:S(2)}) copy-start(bf16[1024,1024]{1,0:T(8,128)(2,1)} %wout_hbm.1) | copy-start | bytes 6291460
  2.7 0.7 %copy-start.1 = (f32[1024]{0:T(1024)S(1)}, f32[1024]{0:T(1024)}, u32[]{:S(2)}) copy-start(f32[1024]{0:T(1024)} %param.6) | copy-start | bytes 12292
  3.4 0.7 %copy-start.2 = (s32[6,8]{1,0:T(8,128)S(1)}, s32[6,8]{1,0:T(8,128)}, u32[]{:S(2)}) copy-start(s32[6,8]{1,0:T(8,128)} %widths_ref.1) | copy-start | bytes 580

commit v2 on v0

--- a/solution.py
+++ b/solution.py
@@ -1,6 +1,8 @@
 import jax
 import jax.numpy as jnp
 from jax import lax
+from jax.experimental import pallas as pl
+from jax.experimental.pallas import tpu as pltpu
 from jax.sharding import PartitionSpec as P
 
 H = 8
@@ -9,6 +11,12 @@
 BLAT = 8
 BLON = 16
 REACH = 2
+D = H * HD
+BLOCK = BLAT * BLON
+GROUP = LATITUDE_BANDS // 2
+CHUNK = BLOCK // 4
+SLOTS = 2 * REACH + 1
+MESH = pl.DeviceIdType.MESH
 
 
 def shifted(array, axis, by):
@@ -105,10 +113,280 @@
     return (x32.reshape(-1, width) + proj).astype(jnp.bfloat16).reshape(lat_rows, lon_tok, width)
 
 
+def fused_kernel(
+    tok_hbm, gain_hbm, wqkv_hbm, wout_hbm, widths_hbm, out_ref,
+    tok, gain, reach, buf, stage, wq, wo, qs, kv, att, back,
+    wsem, x_send, x_recv, o_send, o_recv, c_send, c_recv, r_send, r_recv,
+):
+    n_lon = lax.axis_size("lon")
+    lon, head = lax.axis_index("lon"), lax.axis_index("head")
+    x, core = head // 2, head % 2
+    y = lon % 2
+    turn = 2 * y - 1
+    far = (lax.rem(lon + 2 * turn + n_lon, n_lon), head)
+    near = (lax.rem(lon - 2 * turn + n_lon, n_lon), head)
+    pair = (lon - turn, head)
+    sibling = (lon, 2 * x + 1 - core)
+    across = (lon, 2 * (1 - x) + core)
+    diagonal = (lon, 2 * (1 - x) + 1 - core)
+    partners = [sibling, across, diagonal, far, near, pair]
+    half_cols = H // 2 * HD
+
+    barrier = pltpu.get_barrier_semaphore()
+    for where in partners:
+        pl.semaphore_signal(barrier, inc=1, device_id=where, device_id_type=MESH)
+
+    first = [
+        pltpu.make_async_copy(tok_hbm, tok, wsem.at[4]),
+        pltpu.make_async_copy(gain_hbm, gain, wsem.at[5]),
+    ]
+    loads = []
+    for i in range(3):
+        cols = pl.ds(pl.multiple_of(i * H * HD + core * half_cols, 128), half_cols)
+        loads.append(
+            pltpu.make_async_copy(
+                wqkv_hbm.at[:, cols], wq.at[:, pl.ds(i * half_cols, half_cols)], wsem.at[i]
+            )
+        )
+    loads.append(pltpu.make_async_copy(wout_hbm, wo, wsem.at[3]))
+    loads.append(pltpu.make_async_copy(widths_hbm, reach, wsem.at[6]))
+    for load in first + loads:
+        load.start()
+    for load in first:
+        load.wait()
+
+    def normed(band):
+        part = tok[pl.ds(band * BLAT, BLAT)].astype(jnp.float32).reshape(CHUNK, D)
+        inv = lax.rsqrt(jnp.mean(part * part, axis=-1, keepdims=True) + 1e-05)
+        return (part * inv * gain[...]).astype(jnp.bfloat16)
+
+    def remote(src, dst, send, recv, where):
+        return pltpu.make_async_remote_copy(
+            src_ref=src, dst_ref=dst, send_sem=send, recv_sem=recv,
+            device_id=where, device_id_type=MESH,
+        )
+
+    sent = []
+
+    def begin(copy):
+        copy.start()
+        sent.append(copy)
+        return copy
+
+    def at(slot, j, piece):
+        return buf.at[slot, j, core, x if piece == 0 else 1 - x]
+
+    def move(slot_from, slot_to, j, piece, where):
+        return begin(
+            remote(
+                at(slot_from, j, piece), at(slot_to, j, piece),
+                o_send.at[slot_to, j, piece], o_recv.at[slot_to, j, piece], where,
+            )
+        )
+
+    def share(slot, j):
+        half = buf.at[slot, j, core]
+        return begin(remote(half, half, c_send.at[slot, j], c_recv.at[slot, j], sibling))
+
+    moves = {}
+
+    def spread(j, piece):
+        for slot, where in ((3, far), (2, near), (1, pair)):
+            moves[slot, j, piece] = move(0, slot, j, piece, where)
+
+    crossing = []
+    for j in range(GROUP):
+        stage[j] = normed((1 - x) * GROUP + j)
+        if j == 0:
+            pl.semaphore_wait(barrier, len(partners))
+        crossing.append(
+            begin(remote(stage.at[j], buf.at[0, j, core, x], x_send.at[j], x_recv.at[j], across))
+        )
+        buf[0, j, core, x] = normed(x * GROUP + j)
+        if j == 0:
+            spread(0, 0)
+    shares = []
+    for j in range(GROUP):
+        crossing[j].wait_recv()
+        spread(j, 1)
+        if j + 1 < GROUP:
+            spread(j + 1, 0)
+        shares.append(share(0, j))
+
+    def project(slot, j, with_query):
+        rows = jnp.concatenate(
+            [buf[s, i].reshape(BLOCK, D) for s in slot for i in j], axis=0
+        )
+        start = 0 if with_query else half_cols
+        made = jnp.dot(rows, wq[:, start:], preferred_element_type=jnp.float32).astype(
+            jnp.bfloat16
+        )
+        n = 0
+        for s in slot:
+            for i in j:
+                part = made[n * BLOCK : (n + 1) * BLOCK]
+                if with_query:
+                    qs[i] = part[:, :half_cols]
+                    part = part[:, half_cols:]
+                kv[i, pl.ds(s * BLOCK, BLOCK), :] = part
+                n += 1
+
+    for load in loads[:3]:
+        load.wait()
+    for copy in shares:
+        copy.wait_recv()
+    project((0,), range(GROUP), True)
+    loads[4].wait()
+
+    def relay(j):
+        for piece in range(2):
+            moves[3, j, piece].wait_recv()
+            moves[4, j, piece] = move(3, 4, j, piece, pair)
+        return share(3, j)
+
+    def collect(slot, j):
+        for piece in range(2):
+            moves[slot, j, piece].wait_recv()
+        return share(slot, j)
+
+    def attend(j, h, low, high, dist):
+        cols = pl.ds(h * HD, HD)
+        rows = pl.ds(low * BLOCK, (high - low) * BLOCK)
+        scores = lax.dot_general(
+            qs[j, :, cols], kv[j, rows, cols], (((1,), (1,)), ((), ())),
+            preferred_element_type=jnp.float32,
+        )
+        scores = jnp.where(dist <= reach[x * GROUP + j, lon], scores * HD ** (-0.5), -1e30)
+        top = jnp.max(scores, axis=1, keepdims=True)
+
+        def weigh(new_top):
+            expo = jnp.exp(scores - new_top)
+            value = jnp.dot(
+                expo.astype(jnp.bfloat16), kv[j, rows, pl.ds(half_cols + h * HD, HD)],
+                preferred_element_type=jnp.float32,
+            )
+            return jnp.sum(expo, axis=1, keepdims=True), value
+
+        return top, weigh
+
+    block = lax.broadcasted_iota(jnp.int32, (1, 4 * BLOCK), 1) // BLOCK
+    dist_most = jnp.minimum(block, 2)
+    dist_last = jnp.ones((1, BLOCK), jnp.int32)
+    returns = {}
+
+    def finish(js):
+        bands = [chip * GROUP + j for chip in range(2) for j in js]
+        for j in js:
+            for copy in returns[j]:
+                copy.wait_recv()
+        rows = jnp.concatenate(
+            [
+                jnp.concatenate([back[c, b * CHUNK : (b + 1) * CHUNK] for b in bands], axis=0)
+                for c in range(2)
+            ],
+            axis=1,
+        )
+        proj = jnp.dot(rows, wo[...], preferred_element_type=jnp.float32)
+        for n, b in enumerate(bands):
+            held = tok[b * BLAT : (b + 1) * BLAT].astype(jnp.float32)
+            add = proj[n * CHUNK : (n + 1) * CHUNK].reshape(held.shape)
+            out_ref[b * BLAT : (b + 1) * BLAT] = (held + add).astype(jnp.bfloat16)
+
+    for j in range(GROUP):
+        far_share = relay(j)
+        if j == 0:
+            early = [collect(1, i) for i in range(GROUP)]
+            for copy in early:
+                copy.wait_recv()
+            project((1,), range(GROUP), False)
+        near_share = collect(2, j)
+        far_share.wait_recv()
+        near_share.wait_recv()
+        project((2, 3), (j,), False)
+        states = []
+        for h in range(H // 2):
+            top, weigh = attend(j, h, 0, 4, dist_most)
+            states.append((top, *weigh(top)))
+        if j == GROUP - 1:
+            loads[3].wait()
+            finish(range(GROUP - 1))
+        collect(4, j).wait_recv()
+        project((4,), (j,), False)
+        for h in range(H // 2):
+            top, total, value = states[h]
+            last_top, weigh = attend(j, h, 4, 5, dist_last)
+            new_top = jnp.maximum(top, last_top)
+            factor = jnp.exp(top - new_top)
+            last_total, last_value = weigh(new_top)
+            value = value * factor + last_value
+            total = total * factor + last_total
+            att[j, :, pl.ds(h * HD, HD)] = (value / total).astype(jnp.bfloat16)
+        rows = pl.ds(pl.multiple_of((x * GROUP + j) * CHUNK, CHUNK), CHUNK)
+        returns[j] = []
+        for kind, (where, to_x, to_core) in enumerate(
+            ((across, 1 - x, core), (diagonal, 1 - x, 1 - core), (sibling, x, 1 - core))
+        ):
+            piece = pl.ds(pl.multiple_of((to_core * 2 + to_x) * CHUNK, CHUNK), CHUNK)
+            returns[j].append(
+                begin(
+                    remote(
+                        att.at[j, piece], back.at[core, rows],
+                        r_send.at[j, kind], r_recv.at[j, kind], where,
+                    )
+                )
+            )
+        mine = pl.ds(pl.multiple_of((core * 2 + x) * CHUNK, CHUNK), CHUNK)
+        back[core, rows] = att[j, mine]
+
+    finish((GROUP - 1,))
+    for copy in sent:
+        copy.wait_send()
+
+
+def fused_device(tokens, norm_gain, w_qkv, w_out, widths):
+    lat_rows, lon_tok, width = tokens.shape
+    count = lat_rows * lon_tok
+    half_cols = H // 2 * HD
+    dma = pltpu.SemaphoreType.DMA
+    hbm = pl.BlockSpec(memory_space=pltpu.HBM)
+    return pl.pallas_call(
+        fused_kernel,
+        out_shape=jax.ShapeDtypeStruct(tokens.shape, jnp.bfloat16),
+        in_specs=[hbm] * 5,
+        out_specs=pl.BlockSpec(memory_space=pltpu.VMEM),
+        scratch_shapes=[
+            pltpu.VMEM(tokens.shape, jnp.bfloat16),
+            pltpu.VMEM((1, width), jnp.float32),
+            pltpu.SMEM(widths.shape, jnp.int32),
+            pltpu.VMEM((SLOTS, GROUP, 2, 2, CHUNK, width), jnp.bfloat16),
+            pltpu.VMEM((GROUP, CHUNK, width), jnp.bfloat16),
+            pltpu.VMEM((width, 3 * half_cols), jnp.bfloat16),
+            pltpu.VMEM((width, width), jnp.bfloat16),
+            pltpu.VMEM((GROUP, BLOCK, half_cols), jnp.bfloat16),
+            pltpu.VMEM((GROUP, SLOTS * BLOCK, 2 * half_cols), jnp.bfloat16),
+            pltpu.VMEM((GROUP, BLOCK, half_cols), jnp.bfloat16),
+            pltpu.VMEM((2, count, half_cols), jnp.bfloat16),
+            dma((7,)),
+            dma((GROUP,)),
+            dma((GROUP,)),
+            dma((SLOTS, GROUP, 2)),
+            dma((SLOTS, GROUP, 2)),
+            dma((SLOTS, GROUP)),
+            dma((SLOTS, GROUP)),
+            dma((GROUP, 3)),
+            dma((GROUP, 3)),
+        ],
+        compiler_params=pltpu.CompilerParams(
+            collective_id=0, has_side_effects=True, vmem_limit_bytes=56 * 1024 * 1024
+        ),
+    )(tokens, norm_gain.reshape(1, width), w_qkv, w_out, widths)
+
+
 def solution(mesh):
     placed = (P(None, ("lon", "head"), None), P(), P(), P(), P())
+    one_block = mesh.shape["lon"] == 8 and mesh.shape["head"] == 4
     return jax.shard_map(
-        per_device,
+        fused_device if one_block else per_device,
         mesh=mesh,
         in_specs=placed,
         out_specs=P(None, ("lon", "head"), None),

time: 159 us -> 45.6 us (0.29)
  waiting for transfers between devices: 97.6 us -> 0 us
  Pallas kernels: 0 us -> 43.6 us
  blocking collectives: 19.9 us -> 0 us
  matrix products: 14.1 us -> 0 us
  local copies, waits for them, and re-layouts: 14.1 us -> 1.88 us
  starting transfers between devices: 9.36 us -> 0 us
  other arithmetic: 3.36 us -> 0 us
    ppermute x5 -> x0, waiting for transfers between devices: 90.1 us -> none  [shifted(): lax.ppermute(array, axis, [(i, (i + by) % count) for i in range(count)])]
    pallas_call x0 -> x1, Pallas kernels: none -> 43.6 us  [fused_device(): pl.pallas_call(fused_kernel, out_shape=jax.ShapeDtypeStruct(tokens.shape,...]
    all_to_all x1 -> x0, blocking collectives: 19.9 us -> none  [per_device(): mine = lax.all_to_all(qkv, 'head', split_axis=0, concat_axis=2, tiled=True)]
    dot_general x12 -> x0, matrix products: 14.1 us -> none  [the longest x5 5.28 us: attend(): jnp.einsum('pqtku,pkud->pqtd', expo.astype(jnp.bfloat16), value_entries,...]
    all_to_all x1 -> x0, waiting for transfers between devices: 7.49 us -> none  [per_device(): lax.all_to_all(result, 'head', split_axis=2, concat_axis=0, tiled=True)]
    reshape x5 -> x0, local copies, waits for them, and re-layouts: 6.38 us -> none  [the longest x1 3.36 us: per_device(): qkv = qkv.reshape(LATITUDE_BANDS, BLAT, lon_tok, 3, H, HD).transpose(0, 4...]
    ppermute x5 -> x0, starting transfers between devices: 5.18 us -> none  [shifted(): lax.ppermute(array, axis, [(i, (i + by) % count) for i in range(count)])]
    all_to_all x1 -> x0, starting transfers between devices: 4.17 us -> none  [per_device(): lax.all_to_all(result, 'head', split_axis=2, concat_axis=0, tiled=True)]
  transfers between devices with their start and end apart: 6 -> 0, of which waited for: 6 -> 0; matrix products, arithmetic and copies ran while one was open for 2% -> 0% of each run, Pallas kernels for 0% -> 0%
where the time goes in v2:
time: 45.6 us; the launch traced here: 45.5 us
  Pallas kernels  43.6 us (96%)
  local copies, waits for them, and re-layouts  1.88 us (4%)
    pallas_call x1, Pallas kernels, fused_device(): pl.pallas_call(fused_kernel, out_shape=jax.ShapeDtypeStruct(tokens.shape,...  43.6 us
    unnamed x1, local copies, waits for them, and re-layouts  1.88 us

profile of v2, /device:TPU:0, one launch (start us, length us, event | category | flops | bytes accessed | tf_op | source)
XLA Modules:
  0.0 45.5 jit_solution(11520020151812926014)
XLA Ops:
  0.0 43.6 %shard_map.55 = bf16[48,4,1024]{2,1,0:T(4,128)(2,1)} custom-call(bf16[48,4,1024]{2,1,0:T(4,128)(2,1)} %tok_hbm.1, f32[1,1024]{1,0:T(1,128)} %bitcast.1, bf16[1024,3072]{1,0:T(8,128)(2,1)} %wqkv_hbm.1, bf16[1024,1024]{1,0:T(8,128)(2,1)} %wout_hbm.1, s32[6,8]{1,0:T(8,128)} %widths_hbm.1), custom_call_target="tpu_custom_call" | custom-call | tf_op jit(solution)/shard_map/pallas_call | solution.py:352
  43.6 1.9 %copy.7 = bf16[48,4,1024]{2,1,0:T(4,128)(2,1)} copy(bf16[48,4,1024]{2,1,0:T(4,128)(2,1)} %shard_map.55) | data formatting | bytes 786432

commit v3 on v2

--- a/solution.py
+++ b/solution.py
@@ -191,8 +191,12 @@
     moves = {}
 
     def spread(j, piece):
-        for slot, where in ((3, far), (2, near), (1, pair)):
+        for slot, where in ((2, far), (1, pair)):
             moves[slot, j, piece] = move(0, slot, j, piece, where)
+
+    def spread_near(j):
+        for piece in range(2):
+            moves[3, j, piece] = move(0, 3, j, piece, near)
 
     crossing = []
     for j in range(GROUP):
@@ -203,14 +207,11 @@
             begin(remote(stage.at[j], buf.at[0, j, core, x], x_send.at[j], x_recv.at[j], across))
         )
         buf[0, j, core, x] = normed(x * GROUP + j)
-        if j == 0:
-            spread(0, 0)
+        spread(j, 0)
     shares = []
     for j in range(GROUP):
         crossing[j].wait_recv()
         spread(j, 1)
-        if j + 1 < GROUP:
-            spread(j + 1, 0)
         shares.append(share(0, j))
 
     def project(slot, j, with_query):
@@ -240,9 +241,9 @@
 
     def relay(j):
         for piece in range(2):
-            moves[3, j, piece].wait_recv()
-            moves[4, j, piece] = move(3, 4, j, piece, pair)
-        return share(3, j)
+            moves[2, j, piece].wait_recv()
+            moves[4, j, piece] = move(2, 4, j, piece, pair)
+        return share(2, j)
 
     def collect(slot, j):
         for piece in range(2):
@@ -269,9 +270,9 @@
 
         return top, weigh
 
-    block = lax.broadcasted_iota(jnp.int32, (1, 4 * BLOCK), 1) // BLOCK
-    dist_most = jnp.minimum(block, 2)
-    dist_last = jnp.ones((1, BLOCK), jnp.int32)
+    block = lax.broadcasted_iota(jnp.int32, (1, 3 * BLOCK), 1) // BLOCK
+    dist_early = block
+    dist_late = 2 - block[:, : 2 * BLOCK]
     returns = {}
 
     def finish(js):
@@ -289,38 +290,54 @@
         proj = jnp.dot(rows, wo[...], preferred_element_type=jnp.float32)
         for n, b in enumerate(bands):
             held = tok[b * BLAT : (b + 1) * BLAT].astype(jnp.float32)
-            add = proj[n * CHUNK : (n + 1) * CHUNK].reshape(held.shape)
-            out_ref[b * BLAT : (b + 1) * BLAT] = (held + add).astype(jnp.bfloat16)
-
+            add = proj[n * CHUNK : (n + 1) * CHUNK]
+            out_ref[b * CHUNK : (b + 1) * CHUNK] = (held.reshape(CHUNK, D) + add).astype(
+                jnp.bfloat16
+            )
+
+    states = {}
+
+    def early(j):
+        for h in range(H // 2):
+            top, weigh = attend(j, h, 0, 3, dist_early)
+            states[j, h] = (top, *weigh(top))
+
+    def late(j):
+        for h in range(H // 2):
+            top, total, value = states[j, h]
+            late_top, weigh = attend(j, h, 3, 5, dist_late)
+            new_top = jnp.maximum(top, late_top)
+            factor = jnp.exp(top - new_top)
+            late_total, late_value = weigh(new_top)
+            value = value * factor + late_value
+            total = total * factor + late_total
+            att[j, :, pl.ds(h * HD, HD)] = (value / total).astype(jnp.bfloat16)
+
+    far_shares = []
     for j in range(GROUP):
-        far_share = relay(j)
-        if j == 0:
-            early = [collect(1, i) for i in range(GROUP)]
-            for copy in early:
-                copy.wait_recv()
-            project((1,), range(GROUP), False)
-        near_share = collect(2, j)
-        far_share.wait_recv()
-        near_share.wait_recv()
-        project((2, 3), (j,), False)
-        states = []
-        for h in range(H // 2):
-            top, weigh = attend(j, h, 0, 4, dist_most)
-            states.append((top, *weigh(top)))
-        if j == GROUP - 1:
+        far_shares.append(relay(j))
+        if j > 0:
+            spread_near(j - 1)
+    spread_near(GROUP - 1)
+    pair_shares = [collect(1, j) for j in range(GROUP)]
+    for copy in pair_shares:
+        copy.wait_recv()
+    project((1,), range(GROUP), False)
+    for copy in far_shares:
+        copy.wait_recv()
+    project((2,), range(GROUP), False)
+    early(0)
+    for j in range(GROUP):
+        late_shares = [collect(3, j), collect(4, j)]
+        if j + 1 < GROUP:
+            early(j + 1)
+        else:
             loads[3].wait()
             finish(range(GROUP - 1))
-        collect(4, j).wait_recv()
-        project((4,), (j,), False)
-        for h in range(H // 2):
-            top, total, value = states[h]
-            last_top, weigh = attend(j, h, 4, 5, dist_last)
-            new_top = jnp.maximum(top, last_top)
-            factor = jnp.exp(top - new_top)
-            last_total, last_value = weigh(new_top)
-            value = value * factor + last_value
-            total = total * factor + last_total
-            att[j, :, pl.ds(h * HD, HD)] = (value / total).astype(jnp.bfloat16)
+        for copy in late_shares:
+            copy.wait_recv()
+        project((3, 4), (j,), False)
+        late(j)
         rows = pl.ds(pl.multiple_of((x * GROUP + j) * CHUNK, CHUNK), CHUNK)
         returns[j] = []
         for kind, (where, to_x, to_core) in enumerate(
@@ -349,9 +366,9 @@
     half_cols = H // 2 * HD
     dma = pltpu.SemaphoreType.DMA
     hbm = pl.BlockSpec(memory_space=pltpu.HBM)
-    return pl.pallas_call(
+    out = pl.pallas_call(
         fused_kernel,
-        out_shape=jax.ShapeDtypeStruct(tokens.shape, jnp.bfloat16),
+        out_shape=jax.ShapeDtypeStruct((count, width), jnp.bfloat16),
         in_specs=[hbm] * 5,
         out_specs=pl.BlockSpec(memory_space=pltpu.VMEM),
         scratch_shapes=[
@@ -380,6 +397,7 @@
             collective_id=0, has_side_effects=True, vmem_limit_bytes=56 * 1024 * 1024
         ),
     )(tokens, norm_gain.reshape(1, width), w_qkv, w_out, widths)
+    return out.reshape(lat_rows, lon_tok, width)
 
 
 def solution(mesh):

time: 45.6 us -> 38.5 us (0.84)
  Pallas kernels: 43.6 us -> 36.5 us
    pallas_call x1, Pallas kernels: 43.6 us -> 36.5 us  [fused_device(): pl.pallas_call(fused_kernel, out_shape=jax.ShapeDtypeStruct((count, width...]
    reshape x0 -> x1, local copies, waits for them, and re-layouts: none -> 1.89 us  [fused_device(): return out.reshape(lat_rows, lon_tok, width)]
    unnamed x1 -> x0, local copies, waits for them, and re-layouts: 1.88 us -> none
where the time goes in v3:
time: 38.5 us; the launch traced here: 38.4 us
  Pallas kernels  36.5 us (95%)
  local copies, waits for them, and re-layouts  1.89 us (5%)
    pallas_call x1, Pallas kernels, fused_device(): pl.pallas_call(fused_kernel, out_shape=jax.ShapeDtypeStruct((count, width...  36.5 us
    reshape x1, local copies, waits for them, and re-layouts, fused_device(): return out.reshape(lat_rows, lon_tok, width)  1.89 us

profile of v3, /device:TPU:0, one launch (start us, length us, event | category | flops | bytes accessed | tf_op | source)
XLA Modules:
  0.0 38.4 jit_solution(15647692557515340880)
XLA Ops:
  0.0 36.5 %shard_map.55 = bf16[192,1024]{1,0:T(8,128)(2,1)} custom-call(bf16[48,4,1024]{2,1,0:T(4,128)(2,1)} %tok_hbm.1, f32[1,1024]{1,0:T(1,128)} %bitcast.1, bf16[1024,3072]{1,0:T(8,128)(2,1)} %wqkv_hbm.1, bf16[1024,1024]{1,0:T(8,128)(2,1)} %wout_hbm.1, s32[6,8]{1,0:T(8,128)} %widths_hbm.1), custom_call_target="tpu_custom_call" | custom-call | tf_op jit(solution)/shard_map/pallas_call | solution.py:369
  36.5 1.9 %reshape.7 = bf16[48,4,1024]{2,1,0:T(4,128)(2,1)} reshape(bf16[192,1024]{1,0:T(8,128)(2,1)} %shard_map.55) | data formatting | bytes 786432 | tf_op jit(solution)/shard_map/reshape | solution.py:400

commit v4 on v3

--- a/solution.py
+++ b/solution.py
@@ -316,9 +316,7 @@
     far_shares = []
     for j in range(GROUP):
         far_shares.append(relay(j))
-        if j > 0:
-            spread_near(j - 1)
-    spread_near(GROUP - 1)
+        spread_near(j)
     pair_shares = [collect(1, j) for j in range(GROUP)]
     for copy in pair_shares:
         copy.wait_recv()

time: 38.5 us -> 37.9 us (0.984)
  Pallas kernels: 36.5 us -> 35.8 us
    pallas_call x1, Pallas kernels: 36.5 us -> 35.8 us  [fused_device(): pl.pallas_call(fused_kernel, out_shape=jax.ShapeDtypeStruct((count, width...]
where the time goes in v4:
time: 37.9 us; the launch traced here: 37.7 us
  Pallas kernels  35.8 us (94%)
  local copies, waits for them, and re-layouts  1.89 us (5%)
    pallas_call x1, Pallas kernels, fused_device(): pl.pallas_call(fused_kernel, out_shape=jax.ShapeDtypeStruct((count, width...  35.8 us
    reshape x1, local copies, waits for them, and re-layouts, fused_device(): return out.reshape(lat_rows, lon_tok, width)  1.89 us

profile of v4, /device:TPU:0, one launch (start us, length us, event | category | flops | bytes accessed | tf_op | source)
XLA Modules:
  0.0 37.7 jit_solution(12724016362836083649)
XLA Ops:
  0.0 35.8 %shard_map.55 = bf16[192,1024]{1,0:T(8,128)(2,1)} custom-call(bf16[48,4,1024]{2,1,0:T(4,128)(2,1)} %tok_hbm.1, f32[1,1024]{1,0:T(1,128)} %bitcast.1, bf16[1024,3072]{1,0:T(8,128)(2,1)} %wqkv_hbm.1, bf16[1024,1024]{1,0:T(8,128)(2,1)} %wout_hbm.1, s32[6,8]{1,0:T(8,128)} %widths_hbm.1), custom_call_target="tpu_custom_call" | custom-call | tf_op jit(solution)/shard_map/pallas_call | solution.py:367
  35.8 1.9 %reshape.7 = bf16[48,4,1024]{2,1,0:T(4,128)(2,1)} reshape(bf16[192,1024]{1,0:T(8,128)(2,1)} %shard_map.55) | data formatting | bytes 786432 | tf_op jit(solution)/shard_map/reshape | solution.py:398
